TPU v7x, 32 devices: a whole 2x2x4 slice. The times are simulated.
32 devices in a mesh: group: 1, adapter: 16 (over z, y, core), mp: 2 (over x).
Axes of the slice: x: 2, y: 2, z: 4, core: 2. Of those that a mesh axis runs over, the one named last changes fastest.
Arguments:
- rows: bfloat16 [512, 8192], P(('group', 'adapter'), 'mp'), may hold values from -6 to 6
- request_adapter_index: int32 [512, 1], P(('group', 'adapter')), may hold values from 0 to 15; in each aligned block of 32 rows (0 to 31, 32 to 63, ...) at most 2 rows name the same one
- base_up_matrix: bfloat16 [8192, 14336], P('mp', 'adapter'), may hold values from -0.0625 to 0.0625
- adapter_down_weight: bfloat16 [16, 8192, 64], P('adapter', 'mp'), may hold values from -0.0625 to 0.0625
- adapter_up_weight: bfloat16 [16, 64, 14336], P(None, 'mp', 'adapter'), may hold values from -0.75 to 0.75
Outputs:
- projected: bfloat16 [512, 14336], P(('group', 'mp'), 'adapter')
Inputs may be any that keep to these rules, and one draw needn't show every extreme that they name: `request_adapter_index`: in each aligned block of 32 rows (the rows of one index of adapter) no adapter is named by more than 2 rows, a bound that some block reaches; every adapter is named by some row.
All inputs are finite; a program needn't handle non-finite values.
Results may differ from a plain program's by a relative error of at most 0.0041.
Values may be sent and summed in bfloat16 or wider, within the bound.
A program may use at most 64 MiB of HBM per device.

v0:
```python
import jax
import jax.numpy as jnp
from jax import lax
from jax.sharding import PartitionSpec as P

ADP_DEV = 1
CAP = 2


def body(rows, request_adapter_index, base_up_matrix, adapter_down_weight, adapter_up_weight):
    owners = lax.axis_size("adapter")
    home_rows = rows.shape[0]
    adapter_count_total = adapter_up_weight.shape[0]
    rank_portion = adapter_up_weight.shape[1]
    width_portion = base_up_matrix.shape[1]
    flattened_up_weight = adapter_up_weight.reshape(
        adapter_count_total * rank_portion, width_portion
    )
    base = jnp.dot(
        lax.all_gather(rows, "adapter", axis=0, tiled=True),
        base_up_matrix,
        preferred_element_type=jnp.float32,
    )
    own_ids = request_adapter_index[:, 0]
    target = own_ids // ADP_DEV
    earlier = jnp.tril(jnp.ones((home_rows, home_rows), jnp.int32), -1)
    same_owner = (target[:, None] == target[None, :]).astype(jnp.int32)
    position = jnp.sum(same_owner * earlier, axis=1)
    slot = target * CAP + position
    placing = slot[None, :] == jnp.arange(owners * CAP, dtype=jnp.int32)[:, None]
    placing_values = placing.astype(jnp.bfloat16)
    outbound = jnp.dot(placing_values, rows, preferred_element_type=jnp.float32).astype(
        jnp.bfloat16
    )
    outbound = outbound.reshape(owners, CAP, rows.shape[1])
    slot_ids = jnp.sum(jnp.where(placing, own_ids[None, :] % ADP_DEV + 1, 0), axis=1) - 1
    slot_ids = slot_ids.reshape(owners, CAP)
    got_rows = lax.all_to_all(outbound, "adapter", split_axis=0, concat_axis=0, tiled=True)
    got_ids = lax.all_to_all(slot_ids, "adapter", split_axis=0, concat_axis=0, tiled=True)
    flattened_rows = got_rows.reshape(-1, got_rows.shape[2])
    flat_ids = got_ids.reshape(-1)
    matrix_product = jnp.dot(
        flattened_rows, adapter_down_weight[0], preferred_element_type=jnp.float32
    )
    low = jnp.where((flat_ids == 0)[:, None], matrix_product, 0.0)
    shares = lax.psum_scatter(low, "mp", scatter_dimension=1, tiled=True).astype(jnp.bfloat16)
    shares = shares.reshape(got_rows.shape[0], got_rows.shape[1], shares.shape[1])
    returned = lax.all_to_all(shares, "adapter", split_axis=0, concat_axis=0, tiled=True)
    returned = returned.reshape(owners * CAP, returned.shape[2])
    low_home = jnp.dot(placing_values.T, returned, preferred_element_type=jnp.float32).astype(
        jnp.bfloat16
    )
    low_all, ids_all = (
        lax.all_gather(low_home, "adapter", axis=0, tiled=True),
        lax.all_gather(request_adapter_index, "adapter", axis=0, tiled=True),
    )
    row_ids = ids_all[:, 0]
    marks = row_ids[:, None] == jnp.arange(adapter_count_total, dtype=jnp.int32)[None, :]
    wide = jnp.where(marks[:, :, None], low_all[:, None, :], jnp.zeros((), jnp.bfloat16))
    return lax.psum_scatter(
        base
        + jnp.dot(
            wide.reshape(low_all.shape[0], adapter_count_total * rank_portion),
            flattened_up_weight,
            preferred_element_type=jnp.float32,
        ),
        "mp",
        scatter_dimension=0,
        tiled=True,
    ).astype(jnp.bfloat16)


def solution(mesh):
    return jax.shard_map(
        body,
        mesh=mesh,
        in_specs=(
            P(("group", "adapter"), "mp"),
            P(("group", "adapter"), None),
            P("mp", "adapter"),
            P("adapter", "mp", None),
            P(None, "mp", "adapter"),
        ),
        out_specs=P(("group", "mp"), "adapter"),
        check_vma=False,
    )
```

profile of v0, /device:TPU:0, one launch (start us, length us, event | category | flops | bytes accessed | tf_op | source)
XLA Modules:
  0.0 142.6 jit_solution(11795328305656582369)
XLA Ops:
  7.4 0.9 select_reduce_fusion.1
  8.3 1.2 dynamic-slice
  10.2 0.7 multiply_add_fusion
  11.1 0.7 sub.11
  11.8 7.4 %all-to-all-start = ((s32[16,1,2]{2,1,0:T(1,128)}), s32[16,1,2]{2,1,0:T(1,128)S(1)}, u32[]{:S(2)}, u32[]{:S(2)}) async-start(s32[16,1,2]{2,1,0:T(1,128)} %bitcast.2), calls=%async_computation | async-start | bytes 16384 | tf_op jit(solution)/shard_map/all_to_all | solution.py:39
  19.2 1.2 convolution_convert_fusion
  20.3 0.9 reshape.85
  21.2 4.3 %all-to-all-done = s32[16,1,2]{2,1,0:T(1,128)S(1)} async-done(((s32[16,1,2]{2,1,0:T(1,128)}), s32[16,1,2]{2,1,0:T(1,128)S(1)}, u32[]{:S(2)}, u32[]{:S(2)}) %all-to-all-start) | async-done | bytes 160 | tf_op jit(solution)/shard_map/all_to_all | solution.py:39
  25.6 3.5 %all-to-all-start.1 = ((bf16[16,2,4096]{2,1,0:T(2,128)(2,1)}), bf16[16,2,4096]{2,1,0:T(2,128)(2,1)S(1)}, u32[]{:S(2)}, u32[]{:S(2)}) async-start(bf16[16,2,4096]{2,1,0:T(2,128)(2,1)} %reshape.85), calls=%async_computation.1 | async-start | bytes 524288 | tf_op jit(solution)/shard_map/all_to_all | solution.py:38
  29.3 9.8 %all-to-all-done.1 = bf16[16,2,4096]{2,1,0:T(2,128)(2,1)S(1)} async-done(((bf16[16,2,4096]{2,1,0:T(2,128)(2,1)}), bf16[16,2,4096]{2,1,0:T(2,128)(2,1)S(1)}, u32[]{:S(2)}, u32[]{:S(2)}) %all-to-all-start.1) | async-done | bytes 262176 | tf_op jit(solution)/shard_map/all_to_all | solution.py:38
  39.2 1.3 convolution_select_fusion
  40.5 0.7 copy.10
  41.3 0.5 all-gather.2.cloned.1.call-update
  41.8 9.3 %all-reduce = s32[512]{0:T(512)S(1)} all-reduce(s32[512]{0:T(512)S(1)} %get-tuple-element.6), channel_id=1, replica_groups=mesh['group'=1,'adapter'=16,'mp'=2] {'adapter'}, use_global_device_ids=true, to_apply=%add | all-reduce | flops 512 | bytes 4096
  51.2 1.4 copy.11
  52.6 4.5 %all-to-all-start.2 = ((bf16[16,2,32]{2,1,0:T(2,128)(2,1)}), bf16[16,2,32]{2,1,0:T(2,128)(2,1)S(1)}, u32[]{:S(2)}, u32[]{:S(2)}) async-start(bf16[16,2,32]{2,1,0:T(2,128)(2,1)} %bitcast.4), calls=%async_computation.2 | async-start | bytes 16384 | tf_op jit(solution)/shard_map/all_to_all | solution.py:48
  57.2 6.3 %all-to-all-done.2 = bf16[16,2,32]{2,1,0:T(2,128)(2,1)S(1)} async-done(((bf16[16,2,32]{2,1,0:T(2,128)(2,1)}), bf16[16,2,32]{2,1,0:T(2,128)(2,1)S(1)}, u32[]{:S(2)}, u32[]{:S(2)}) %all-to-all-start.2) | async-done | bytes 2080 | tf_op jit(solution)/shard_map/all_to_all | solution.py:48
  63.4 0.2 convolution_convert_fusion.1
  63.6 18.4 %all_gather.14 = bf16[512,32]{1,0:T(8,128)(2,1)S(1)} all-gather(bf16[32,32]{1,0:T(8,128)(2,1)S(1)} %convolution_convert_fusion.1), channel_id=1, replica_groups=mesh['group'=1,'adapter'=16,'mp'=2] {'adapter'}, dimensions={0}, use_global_device_ids=true | all-gather | bytes 34816 | tf_op jit(solution)/shard_map/all_gather | solution.py:54
  82.1 10.4 %all-gather.2.cloned.1.call-done = bf16[512,4096]{1,0:T(8,128)(2,1)} async-done(((bf16[32,4096]{1,0:T(8,128)(2,1)}), bf16[512,4096]{1,0:T(8,128)(2,1)}) %all-gather.2.cloned.1.call-update) | async-done | bytes 4194320 | tf_op jit(solution)/shard_map/all_gather | solution.py:20
  92.6 10.1 %fusion.8 = f32[512,896]{1,0:T(8,128)S(1)} fusion(bf16[512,4096]{1,0:T(8,128)(2,1)} %all-gather.2.cloned.1.call-done, bf16[4096,896]{1,0:T(8,128)(2,1)} %param.7), kind=kOutput, calls=%fused_computation.22 | convolution fusion | flops 3758096384 | bytes 13369344 | tf_op jit(solution)/shard_map/dot_general | solution.py:19
  102.7 2.0 %bitcast_add_fusion = f32[512,896]{1,0:T(8,128)} fusion(f32[512,896]{1,0:T(8,128)S(1)} %fusion.8, bf16[16,32,896]{2,1,0:T(8,128)(2,1)S(1)} %copy-done, pred[512,16]{0,1:T(8,128)(4,1)S(1)} %iota_compare_fusion, bf16[512,32]{0,1:T(8,128)(2,1)S(1)} %copy.9), kind=kOutput, calls=%fused_computation.1 | convolution fusion | flops 470482944 | bytes 4628480 | tf_op jit(solution)/shard_map/dot_general | solution.py:62
  104.7 28.5 %reduce-scatter.5.cloned.1.call-done = f32[256,896]{1,0:T(8,128)} async-done(((f32[512,896]{1,0:T(8,128)}), f32[256,896]{1,0:T(8,128)}) %reduce-scatter.5.cloned.1.call-update) | async-done | bytes 917520 | tf_op jit(solution)/shard_map/reduce_scatter | solution.py:60
  133.2 2.0 %convert_element_type.17 = bf16[256,896]{1,0:T(8,128)(2,1)} convert(f32[256,896]{1,0:T(8,128)} %reduce-scatter.5.cloned.1.call-done) | non-fusion elementwise | flops 229376 | bytes 1376256 | tf_op jit(solution)/shard_map/convert_element_type | solution.py:70
  (17 shorter events, 0.6 us)
Async XLA Ops:
  7.4 95.3 %copy-start = (bf16[16,32,896]{2,1,0:T(8,128)(2,1)S(1)}, bf16[16,32,896]{2,1,0:T(8,128)(2,1)}, u32[]{:S(2)}) copy-start(bf16[16,32,896]{2,1,0:T(8,128)(2,1)} %param.9) | copy-start | bytes 2752516
  11.8 13.8 %all-to-all-start = ((s32[16,1,2]{2,1,0:T(1,128)}), s32[16,1,2]{2,1,0:T(1,128)S(1)}, u32[]{:S(2)}, u32[]{:S(2)}) async-start(s32[16,1,2]{2,1,0:T(1,128)} %bitcast.2), calls=%async_computation | async-start | bytes 16384 | tf_op jit(solution)/shard_map/all_to_all | solution.py:39
  25.6 13.5 %all-to-all-start.1 = ((bf16[16,2,4096]{2,1,0:T(2,128)(2,1)}), bf16[16,2,4096]{2,1,0:T(2,128)(2,1)S(1)}, u32[]{:S(2)}, u32[]{:S(2)}) async-start(bf16[16,2,4096]{2,1,0:T(2,128)(2,1)} %reshape.85), calls=%async_computation.1 | async-start | bytes 524288 | tf_op jit(solution)/shard_map/all_to_all | solution.py:38
  29.1 22.1 %reduce-scatter.7.cloned.1.call-start = ((), (), s32[]{:S(2)}) async-start(), calls=%async_computation.7 | async-start | bytes 49152
  41.3 51.3 %all-gather.2.cloned.1.call-start = ((), (), s32[]{:S(2)}) async-start(), calls=%async_computation.5 | async-start | bytes 4456448 | tf_op jit(solution)/shard_map/all_gather | solution.py:20
  52.6 10.9 %all-to-all-start.2 = ((bf16[16,2,32]{2,1,0:T(2,128)(2,1)}), bf16[16,2,32]{2,1,0:T(2,128)(2,1)S(1)}, u32[]{:S(2)}, u32[]{:S(2)}) async-start(bf16[16,2,32]{2,1,0:T(2,128)(2,1)} %bitcast.4), calls=%async_computation.2 | async-start | bytes 16384 | tf_op jit(solution)/shard_map/all_to_all | solution.py:48
  57.1 76.1 %reduce-scatter.5.cloned.1.call-start = ((), (), s32[]{:S(2)}) async-start(), calls=%async_computation.6 | async-start | bytes 2752512 | tf_op jit(solution)/shard_map/reduce_scatter | solution.py:60
Sparse Core Ops, SparseCore 0:
  41.4 8.0 reduce-scatter.6
  104.8 28.3 reduce-scatter.4
Sparse Core Ops, SparseCore 1:
  43.9 48.6 all-gather.1
where the time goes:
time: 143 us
  waiting for transfers between devices  60 us (42%)
  blocking collectives  27.8 us (19%)
  starting transfers between devices  15.6 us (11%)
  between operations  15.6 us (11%)
  matrix products  14.7 us (10%)
  local copies, waits for them, and re-layouts  5.21 us (4%)
  other arithmetic  3.84 us (3%)
    reduce_scatter x1, waiting for transfers between devices, body(): lax.psum_scatter(base + jnp.dot(wide.reshape(low_all.shape[0], adapter_co...  28.5 us
    all_gather x1, blocking collectives, body(): lax.all_gather(low_home, 'adapter', axis=0, tiled=True)  18.4 us
    all_gather x1, waiting for transfers between devices, body(): lax.all_gather(rows, 'adapter', axis=0, tiled=True)  10.4 us
    dot_general x1, matrix products, body(): jnp.dot(lax.all_gather(rows, 'adapter', axis=0, tiled=True), base_up_matr...  10.1 us
    all_to_all x1, waiting for transfers between devices, body(): lax.all_to_all(outbound, 'adapter', split_axis=0, concat_axis=0, tiled=True)  9.82 us
    unnamed x1, blocking collectives  9.34 us
    all_to_all x1, starting transfers between devices, body(): lax.all_to_all(slot_ids, 'adapter', split_axis=0, concat_axis=0, tiled=True)  7.39 us
    all_to_all x1, waiting for transfers between devices, body(): lax.all_to_all(shares, 'adapter', split_axis=0, concat_axis=0, tiled=True)  6.27 us
  transfers between devices with their start and end apart: 6, of which 5 were waited for; matrix products, arithmetic and copies ran while one was open for 3% of the time, Pallas kernels for 0%

commit v1 on v0

v1 whole, which is shorter than its diff:
```python
import functools

import jax
import jax.numpy as jnp
from jax import lax
from jax.experimental import pallas as pl
from jax.experimental.pallas import tpu as pltpu
from jax.sharding import PartitionSpec as P

CAP = 2
MESH = pl.DeviceIdType.MESH
F32 = jnp.float32
BF16 = jnp.bfloat16


def iota(shape, dim):
    return lax.broadcasted_iota(jnp.int32, shape, dim)


def kernel(
    dims, rows, ids, base, down, up, out,
    xg, w, dw, uw, acc, plow, slots, slot_row, part, part_in, low_own, low_all, sbuf, rbuf,
    lsem, ring_s, ring_r, sib_s, sib_r, slot_s, slot_r, part_s, part_r, low_s, low_r, out_s, out_r,
):
    owners, parts, folded = dims
    chips = owners // 2
    far = chips // 2
    home, features = rows.shape
    half = home // 2
    width = base.shape[1]
    rank = down.shape[1]
    rank_portion = up.shape[0] // owners
    total = owners * home
    mine = CAP * owners
    share = total // parts
    chunk = 128

    me = lax.axis_index("adapter")
    m = lax.axis_index("mp")
    core = lax.rem(me, 2)
    chip = me // 2
    if folded:
        y, z = lax.rem(chip, 2), chip // 2
        place = z + y * (chips - 1 - 2 * z)
    else:
        place = chip

    def device_at(q, c):
        q = lax.rem(q + 2 * chips, chips)
        if folded:
            y = q // (chips // 2)
            q = 2 * (q + y * (chips - 1 - 2 * q)) + y
        return 2 * q + c

    sibling = me + 1 - 2 * core
    ahead = (device_at(place + 1, core), device_at(place - 1, core))

    def peer(d):
        return lax.rem(me + d, owners)

    loads = [
        pltpu.make_async_copy(rows, xg.at[pl.ds(0, home)], lsem.at[0]),
        pltpu.make_async_copy(base, w, lsem.at[1]),
        pltpu.make_async_copy(down, dw, lsem.at[2]),
        pltpu.make_async_copy(up, uw, lsem.at[3]),
    ]
    for copy in loads:
        copy.start()

    barrier = pltpu.get_barrier_semaphore()

    def greet(d, _):
        pl.semaphore_signal(barrier, inc=1, device_id={"adapter": peer(d)}, device_id_type=MESH)
        return 0

    lax.fori_loop(1, owners, greet, 0)
    for d in range(1, parts):
        pl.semaphore_signal(barrier, inc=1, device_id={"mp": lax.rem(m + d, parts)}, device_id_type=MESH)

    lane = iota((home, 128), 1)
    row = iota((home, 128), 0)
    column = jnp.broadcast_to(ids[...], (home, 128)).astype(F32)
    inner = lax.rem(lane, home)
    across = jnp.sum(jnp.where(inner == row, column, 0.0), axis=0, keepdims=True)
    before = jnp.where((column == across) & (row < inner), 1.0, 0.0)
    position = jnp.sum(before, axis=0, keepdims=True)
    slot = across * mine + position + (CAP * me + 1).astype(F32)
    group_of = 128 // home
    here = iota((1, 128), 1) // home == lax.rem(me, group_of)
    slots[me] = jnp.broadcast_to(jnp.where(here, slot, 0.0), (8, 128))

    pl.semaphore_wait(barrier, owners - 1 + parts - 1)

    def reach(d, h):
        return far if d == h else far - 1

    def at(k, d, s, h):
        if k == 0:
            start = 0
        else:
            start = 2 * home + (k - 1) * 4 * home + (d * 2 * home if k < far else 0)
        return pl.ds(start + s * home + h * half, half)

    def ring(k, d, h):
        src = rows.at[pl.ds(h * half, half)] if k == 1 else xg.at[at(k - 1, d, 0, h)]
        return pltpu.make_async_remote_copy(
            src_ref=src, dst_ref=xg.at[at(k, d, 0, h)],
            send_sem=ring_s.at[d, k, h], recv_sem=ring_r.at[d, k, h],
            device_id={"adapter": ahead[d]}, device_id_type=MESH,
        )

    def across_chip(k, d, h):
        src = rows.at[pl.ds(h * half, half)] if k == 0 else xg.at[at(k, d, 0, h)]
        return pltpu.make_async_remote_copy(
            src_ref=src, dst_ref=xg.at[at(k, d, 1, h)],
            send_sem=sib_s.at[d, k, h], recv_sem=sib_r.at[d, k, h],
            device_id={"adapter": sibling}, device_id_type=MESH,
        )

    def slot_copy(d):
        return pltpu.make_async_remote_copy(
            src_ref=slots.at[me], dst_ref=slots.at[me],
            send_sem=slot_s.at[d], recv_sem=slot_r.at[d],
            device_id={"adapter": peer(d)}, device_id_type=MESH,
        )

    def low_copy(d):
        return pltpu.make_async_remote_copy(
            src_ref=low_own, dst_ref=low_all.at[pl.ds(pl.multiple_of(me * mine, mine), mine)],
            send_sem=low_s.at[d], recv_sem=low_r.at[d],
            device_id={"adapter": peer(d)}, device_id_type=MESH,
        )

    def each_peer(action):
        def go(d, _):
            action(d)
            return 0

        lax.fori_loop(1, owners, go, 0)

    for h in range(2):
        for d in range(2):
            ring(1, d, h).start()
    for h in range(2):
        across_chip(0, 0, h).start()
    each_peer(lambda d: slot_copy(d).start())

    def region(k):
        count = 2 * home if k in (0, far) else 4 * home
        start = 0 if k == 0 else 2 * home + (k - 1) * 4 * home
        origins = []
        for d in range(count // (2 * home)):
            q = place - k if d == 0 else place + k
            origins += [device_at(q, core), device_at(q, 1 - core)]
        return start, count, [pl.multiple_of(o * home, home) for o in origins]

    def low_part(k):
        start, count, origins = region(k)
        r = jnp.dot(xg[start:start + count, :], dw[...], preferred_element_type=F32)
        for i, o in enumerate(origins):
            plow[pl.ds(o, home), :] = r[i * home:(i + 1) * home]

    def base_part(k):
        start, count, origins = region(k)
        for n in range(0, width, 256):
            e = min(n + 256, width)
            r = jnp.dot(xg[start:start + count, :], w[:, n:e], preferred_element_type=F32)
            for i, o in enumerate(origins):
                acc[pl.ds(o, home), n:e] = r[i * home:(i + 1) * home]

    def siblings_in(k):
        for h in range(2):
            for d in range(2):
                if (k == 0 and d == 0) or (k > 0 and k <= reach(d, h)):
                    across_chip(k, d, h).wait_recv()

    for k in range(1, far + 1):
        for h in range(2):
            for d in range(2):
                if k <= reach(d, h):
                    ring(k, d, h).wait_recv()
                    if k + 1 <= reach(d, h):
                        ring(k + 1, d, h).start()
                    across_chip(k, d, h).start()
        if k == 1:
            for copy in loads[:3]:
                copy.wait()
        siblings_in(k - 1)
        low_part(k - 1)
        base_part(k - 1)
    siblings_in(far)
    low_part(far)

    each_peer(lambda d: slot_copy(d).wait_recv())
    for q in range(total // 128):
        line = slots[q * group_of]
        for i in range(1, group_of):
            line = line + slots[q * group_of + i]
        slot_row[:, q * 128:(q + 1) * 128] = line
    wanted = (iota((mine, total), 0) + (me * mine + 1)).astype(F32)
    pick = jnp.where(wanted == slot_row[0:1, :], 1.0, 0.0)
    part[...] = jnp.dot(pick, plow[...], preferred_element_type=F32, precision=lax.Precision.HIGHEST)

    def part_copy(d):
        return pltpu.make_async_remote_copy(
            src_ref=part, dst_ref=part_in.at[d - 1],
            send_sem=part_s.at[d], recv_sem=part_r.at[d],
            device_id={"mp": lax.rem(m + d, parts)}, device_id_type=MESH,
        )

    for d in range(1, parts):
        part_copy(d).start()
    base_part(far)
    low = part[...]
    for d in range(1, parts):
        part_copy(d).wait_recv()
        low = low + part_in[d - 1]
    low_own[...] = jnp.broadcast_to(me.astype(F32), (mine, 128)).astype(BF16)
    low_own[:, :rank] = low.astype(BF16)
    each_peer(lambda d: low_copy(d).start())
    low_all[pl.ds(pl.multiple_of(me * mine, mine), mine), :] = low_own[...]
    spread = jnp.where(
        iota((128, owners * rank_portion), 0)
        == m * rank_portion + lax.rem(iota((128, owners * rank_portion), 1), rank_portion),
        1.0, 0.0,
    ).astype(BF16)
    of_column = (iota((chunk, owners * rank_portion), 1) // rank_portion).astype(F32)
    loads[3].wait()
    each_peer(lambda d: low_copy(d).wait_recv())

    def finished(first):
        all_slots = (iota((owners * mine, chunk), 0) + 1).astype(F32)
        hit = jnp.where(all_slots == slot_row[0:1, pl.ds(first, chunk)], 1.0, 0.0).astype(BF16)
        low_rows = lax.dot_general(
            hit, low_all[...], (((0,), (0,)), ((), ())), preferred_element_type=F32
        )
        copies = jnp.dot(low_rows.astype(BF16), spread, preferred_element_type=F32)
        wide = jnp.where(of_column == low_rows[:, rank:rank + 1], copies, 0.0).astype(BF16)
        return acc[pl.ds(first, chunk), :] + jnp.dot(wide, uw[...], preferred_element_type=F32)

    def out_copy(d, c):
        return pltpu.make_async_remote_copy(
            src_ref=sbuf.at[d - 1, c], dst_ref=rbuf.at[d - 1, c],
            send_sem=out_s.at[d, c], recv_sem=out_r.at[d, c],
            device_id={"mp": lax.rem(m + d, parts)}, device_id_type=MESH,
        )

    pieces = share // chunk
    for d in range(1, parts):
        to = lax.rem(m + d, parts)
        for c in range(pieces):
            sbuf[d - 1, c] = finished(pl.multiple_of(to * share + c * chunk, chunk)).astype(BF16)
            out_copy(d, c).start()
    for c in range(pieces):
        first = pl.multiple_of(m * share + c * chunk, chunk)
        acc[pl.ds(first, chunk), :] = finished(first)
    for c in range(pieces):
        value = acc[pl.ds(pl.multiple_of(m * share + c * chunk, chunk), chunk), :]
        for d in range(1, parts):
            out_copy(d, c).wait_recv()
            value = value + rbuf[d - 1, c].astype(F32)
        out[c * chunk:(c + 1) * chunk, :] = value.astype(BF16)

    for h in range(2):
        for d in range(2):
            for k in range(1, reach(d, h) + 1):
                ring(k, d, h).wait_send()
                across_chip(k, d, h).wait_send()
        across_chip(0, 0, h).wait_send()
    each_peer(lambda d: slot_copy(d).wait_send())
    each_peer(lambda d: low_copy(d).wait_send())
    for d in range(1, parts):
        part_copy(d).wait_send()
        for c in range(pieces):
            out_copy(d, c).wait_send()


def solution(mesh):
    owners, parts = mesh.shape["adapter"], mesh.shape["mp"]
    folded = mesh.shape["group"] == 1

    def body(rows, request_adapter_index, base_up_matrix, adapter_down_weight, adapter_up_weight):
        home, features = rows.shape
        width = base_up_matrix.shape[1]
        rank = adapter_down_weight.shape[2]
        rank_portion = adapter_up_weight.shape[1]
        total = owners * home
        mine = CAP * owners
        share = total // parts
        pieces = share // 128
        far = owners // 4
        any_space = pl.BlockSpec(memory_space=pl.ANY)
        in_vmem = pl.BlockSpec(memory_space=pltpu.VMEM)
        dma = pltpu.SemaphoreType.DMA
        flops = 2 * total * features * (width + rank)
        return pl.pallas_call(
            functools.partial(kernel, (owners, parts, folded)),
            out_shape=jax.ShapeDtypeStruct((share, width), BF16),
            in_specs=[any_space, in_vmem, any_space, any_space, any_space],
            out_specs=in_vmem,
            scratch_shapes=[
                pltpu.VMEM((total, features), BF16),
                pltpu.VMEM((features, width), BF16),
                pltpu.VMEM((features, rank), BF16),
                pltpu.VMEM((owners * rank_portion, width), BF16),
                pltpu.VMEM((total, width), F32),
                pltpu.VMEM((total, rank), F32),
                pltpu.VMEM((owners, 8, 128), F32),
                pltpu.VMEM((8, total), F32),
                pltpu.VMEM((mine, rank), F32),
                pltpu.VMEM((parts - 1, mine, rank), F32),
                pltpu.VMEM((mine, 128), BF16),
                pltpu.VMEM((owners * mine, 128), BF16),
                pltpu.VMEM((parts - 1, pieces, 128, width), BF16),
                pltpu.VMEM((parts - 1, pieces, 128, width), BF16),
                dma((4,)),
                dma((2, far + 1, 2)),
                dma((2, far + 1, 2)),
                dma((2, far + 1, 2)),
                dma((2, far + 1, 2)),
                dma((owners,)),
                dma((owners,)),
                dma((parts,)),
                dma((parts,)),
                dma((owners,)),
                dma((owners,)),
                dma((parts, pieces)),
                dma((parts, pieces)),
            ],
            compiler_params=pltpu.CompilerParams(
                collective_id=0, has_side_effects=True, vmem_limit_bytes=56 * 1024 * 1024
            ),
            cost_estimate=pl.CostEstimate(
                flops=flops, bytes_accessed=2 * features * width, transcendentals=0
            ),
        )(
            rows,
            request_adapter_index,
            base_up_matrix,
            adapter_down_weight.reshape(features, rank),
            adapter_up_weight.reshape(owners * rank_portion, width),
        )

    return jax.shard_map(
        body,
        mesh=mesh,
        in_specs=(
            P(("group", "adapter"), "mp"),
            P(("group", "adapter"), None),
            P("mp", "adapter"),
            P("adapter", "mp", None),
            P(None, "mp", "adapter"),
        ),
        out_specs=P(("group", "mp"), "adapter"),
        check_vma=False,
    )
```

time: 143 us -> 60.3 us (0.42)
  waiting for transfers between devices: 60 us -> 0 us
  Pallas kernels: 0 us -> 54.5 us
  blocking collectives: 27.8 us -> 0 us
  starting transfers between devices: 15.6 us -> 0 us
  between operations: 15.6 us -> 0.01 us
  matrix products: 14.7 us -> 0 us
  other arithmetic: 3.84 us -> 0 us
    pallas_call x0 -> x1, Pallas kernels: none -> 54.5 us  [body(): pl.pallas_call(functools.partial(kernel, (owners, parts, folded)), out_sh...]
    reduce_scatter x1 -> x0, waiting for transfers between devices: 28.5 us -> none  [body(): lax.psum_scatter(base + jnp.dot(wide.reshape(low_all.shape[0], adapter_co...]
    all_to_all x3 -> x0, waiting for transfers between devices: 20.4 us -> none  [the longest x1 9.82 us: body(): lax.all_to_all(outbound, 'adapter', split_axis=0, concat_axis=0, tiled=True)]
    all_gather x1 -> x0, blocking collectives: 18.4 us -> none  [body(): lax.all_gather(low_home, 'adapter', axis=0, tiled=True)]
    all_to_all x3 -> x0, starting transfers between devices: 15.4 us -> none  [the longest x1 7.39 us: body(): lax.all_to_all(slot_ids, 'adapter', split_axis=0, concat_axis=0, tiled=True)]
    dot_general x5 -> x0, matrix products: 14.7 us -> none  [the longest x1 10.1 us: body(): jnp.dot(lax.all_gather(rows, 'adapter', axis=0, tiled=True), base_up_matr...]
    all_gather x1 -> x0, waiting for transfers between devices: 10.4 us -> none  [body(): lax.all_gather(rows, 'adapter', axis=0, tiled=True)]
    unnamed x1 -> x0, blocking collectives: 9.34 us -> none
  transfers between devices with their start and end apart: 6 -> 0, of which waited for: 5 -> 0; matrix products, arithmetic and copies ran while one was open for 3% -> 0% of each run, Pallas kernels for 0% -> 0%
where the time goes in v1:
time: 60.3 us; the launch traced here: 60.1 us
  Pallas kernels  54.5 us (90%)
  local copies, waits for them, and re-layouts  5.54 us (9%)
    pallas_call x1, Pallas kernels, body(): pl.pallas_call(functools.partial(kernel, (owners, parts, folded)), out_sh...  54.5 us
    unnamed x3, local copies, waits for them, and re-layouts  5.54 us

profile of v1, /device:TPU:0, one launch (start us, length us, event | category | flops | bytes accessed | tf_op | source)
XLA Modules:
  0.0 60.1 jit_solution(4540048002708355418)
XLA Ops:
  0.0 1.3 %copy.7.ids = s32[32,1]{1,0:T(8,128)} copy(s32[32,1]{0,1:T(1,128)} %param.6) | data formatting | bytes 256 | tf_op args[1]
  1.3 2.4 %copy.6 = bf16[1,4096,64]{2,1,0:T(8,128)(2,1)} copy(bf16[1,4096,64]{1,2,0:T(8,128)(2,1)} %param.8) | data formatting | bytes 1048576 | tf_op args[3]
  3.7 54.5 %shard_map.55 = bf16[256,896]{1,0:T(8,128)(2,1)} custom-call(bf16[32,4096]{1,0:T(8,128)(2,1)} %rows.1, s32[32,1]{1,0:T(8,128)} %copy.7.ids, bf16[4096,896]{1,0:T(8,128)(2,1)} %base.1, bf16[4096,64]{1,0:T(8,128)(2,1)} %bitcast.2, bf16[512,896]{1,0:T(8,128)(2,1)} %bitcast.3), custom_call_target="tpu_custom_call" | custom-call | flops 4026531840 | bytes 7340032 | tf_op jit(solution)/shard_map/pallas_call | solution.py:296
  58.3 1.8 %copy.9 = bf16[256,896]{1,0:T(8,128)(2,1)} copy(bf16[256,896]{1,0:T(8,128)(2,1)} %shard_map.55) | data formatting | bytes 917504

commit v2 on v1

--- a/solution.py
+++ b/solution.py
@@ -20,7 +20,7 @@
 def kernel(
     dims, rows, ids, base, down, up, out,
     xg, w, dw, uw, acc, plow, slots, slot_row, part, part_in, low_own, low_all, sbuf, rbuf,
-    lsem, ring_s, ring_r, sib_s, sib_r, slot_s, slot_r, part_s, part_r, low_s, low_r, out_s, out_r,
+    lsem, ring_s, ring_r, sib_s, sib_r, slot_s, slot_r, part_s, part_r, low_s, low_r, out_s, out_r, up_s, up_r,
 ):
     owners, parts, folded = dims
     chips = owners // 2
@@ -28,12 +28,14 @@
     home, features = rows.shape
     half = home // 2
     width = base.shape[1]
-    rank = down.shape[1]
+    rank = down.shape[0]
     rank_portion = up.shape[0] // owners
     total = owners * home
     mine = CAP * owners
     share = total // parts
     chunk = 128
+    some = mine // parts
+    part_chips = chips // parts
 
     me = lax.axis_index("adapter")
     m = lax.axis_index("mp")
@@ -62,7 +64,7 @@
         pltpu.make_async_copy(rows, xg.at[pl.ds(0, home)], lsem.at[0]),
         pltpu.make_async_copy(base, w, lsem.at[1]),
         pltpu.make_async_copy(down, dw, lsem.at[2]),
-        pltpu.make_async_copy(up, uw, lsem.at[3]),
+        pltpu.make_async_copy(up, uw.at[0], lsem.at[3]),
     ]
     for copy in loads:
         copy.start()
@@ -79,7 +81,10 @@
 
     lane = iota((home, 128), 1)
     row = iota((home, 128), 0)
-    column = jnp.broadcast_to(ids[...], (home, 128)).astype(F32)
+    square = jnp.broadcast_to(ids[...].astype(F32), (home, home))
+    diagonal = iota((home, home), 0) == iota((home, home), 1)
+    column = jnp.sum(jnp.where(diagonal, square, 0.0), axis=1, keepdims=True)
+    column = jnp.broadcast_to(column, (home, 128))
     inner = lax.rem(lane, home)
     across = jnp.sum(jnp.where(inner == row, column, 0.0), axis=0, keepdims=True)
     before = jnp.where((column == across) & (row < inner), 1.0, 0.0)
@@ -126,7 +131,7 @@
 
     def low_copy(d):
         return pltpu.make_async_remote_copy(
-            src_ref=low_own, dst_ref=low_all.at[pl.ds(pl.multiple_of(me * mine, mine), mine)],
+            src_ref=low_own, dst_ref=low_all.at[pl.ds(pl.multiple_of(me * some, some), some)],
             send_sem=low_s.at[d], recv_sem=low_r.at[d],
             device_id={"adapter": peer(d)}, device_id_type=MESH,
         )
@@ -144,6 +149,33 @@
     for h in range(2):
         across_chip(0, 0, h).start()
     each_peer(lambda d: slot_copy(d).start())
+
+    def up_copy(d):
+        return pltpu.make_async_remote_copy(
+            src_ref=up, dst_ref=uw.at[d],
+            send_sem=up_s.at[d], recv_sem=up_r.at[d],
+            device_id={"mp": lax.rem(m + d, parts)}, device_id_type=MESH,
+        )
+
+    for d in range(1, parts):
+        up_copy(d).start()
+
+    def out_copy(c, to, d):
+        local = pl.ds(pl.multiple_of(lax.rem(c, part_chips) * 2 * home, 2 * home), 2 * home)
+        return pltpu.make_async_remote_copy(
+            src_ref=sbuf.at[c], dst_ref=rbuf.at[d - 1, local],
+            send_sem=out_s.at[c], recv_sem=out_r.at[d - 1, lax.rem(c, part_chips)],
+            device_id={"mp": to}, device_id_type=MESH,
+        )
+
+    def send_part(c):
+        to = c // part_chips
+
+        @pl.when(to != m)
+        def _():
+            rows_of = pl.ds(pl.multiple_of(c * 2 * home, 2 * home), 2 * home)
+            sbuf[c] = acc[rows_of, :].astype(BF16)
+            out_copy(c, to, lax.rem(to - m + parts, parts)).start()
 
     def region(k):
         count = 2 * home if k in (0, far) else 4 * home
@@ -156,7 +188,10 @@
 
     def low_part(k):
         start, count, origins = region(k)
-        r = jnp.dot(xg[start:start + count, :], dw[...], preferred_element_type=F32)
+        r = lax.dot_general(
+            xg[start:start + count, :], dw[...], (((1,), (1,)), ((), ())),
+            preferred_element_type=F32,
+        )
         for i, o in enumerate(origins):
             plow[pl.ds(o, home), :] = r[i * home:(i + 1) * home]
 
@@ -167,6 +202,8 @@
             r = jnp.dot(xg[start:start + count, :], w[:, n:e], preferred_element_type=F32)
             for i, o in enumerate(origins):
                 acc[pl.ds(o, home), n:e] = r[i * home:(i + 1) * home]
+        for o in origins[::2]:
+            send_part(o // (2 * home))
 
     def siblings_in(k):
         for h in range(2):
@@ -201,64 +238,59 @@
     pick = jnp.where(wanted == slot_row[0:1, :], 1.0, 0.0)
     part[...] = jnp.dot(pick, plow[...], preferred_element_type=F32, precision=lax.Precision.HIGHEST)
 
+    def own_part(q):
+        return pl.ds(pl.multiple_of(q * some, some), some)
+
     def part_copy(d):
-        return pltpu.make_async_remote_copy(
-            src_ref=part, dst_ref=part_in.at[d - 1],
+        to = lax.rem(m + d, parts)
+        return pltpu.make_async_remote_copy(
+            src_ref=part.at[own_part(to)], dst_ref=part_in.at[d - 1],
             send_sem=part_s.at[d], recv_sem=part_r.at[d],
-            device_id={"mp": lax.rem(m + d, parts)}, device_id_type=MESH,
+            device_id={"mp": to}, device_id_type=MESH,
         )
 
     for d in range(1, parts):
         part_copy(d).start()
     base_part(far)
-    low = part[...]
+    low = part[own_part(m), :]
     for d in range(1, parts):
         part_copy(d).wait_recv()
         low = low + part_in[d - 1]
-    low_own[...] = jnp.broadcast_to(me.astype(F32), (mine, 128)).astype(BF16)
+    low_own[...] = jnp.broadcast_to(me.astype(F32), (some, 128)).astype(BF16)
     low_own[:, :rank] = low.astype(BF16)
     each_peer(lambda d: low_copy(d).start())
-    low_all[pl.ds(pl.multiple_of(me * mine, mine), mine), :] = low_own[...]
-    spread = jnp.where(
-        iota((128, owners * rank_portion), 0)
-        == m * rank_portion + lax.rem(iota((128, owners * rank_portion), 1), rank_portion),
-        1.0, 0.0,
-    ).astype(BF16)
+    low_all[own_part(me), :] = low_own[...]
+    wide_shape = (128, owners * rank_portion)
+    within = lax.rem(iota(wide_shape, 1), rank_portion)
     of_column = (iota((chunk, owners * rank_portion), 1) // rank_portion).astype(F32)
+    ordinal = iota((owners * some, chunk), 0)
+    all_slots = (ordinal // some * mine + m * some + lax.rem(ordinal, some) + 1).astype(F32)
     loads[3].wait()
+    for d in range(1, parts):
+        up_copy(d).wait_recv()
     each_peer(lambda d: low_copy(d).wait_recv())
 
-    def finished(first):
-        all_slots = (iota((owners * mine, chunk), 0) + 1).astype(F32)
+    pieces = share // chunk
+    for c in range(pieces):
+        first = pl.multiple_of(m * share + c * chunk, chunk)
         hit = jnp.where(all_slots == slot_row[0:1, pl.ds(first, chunk)], 1.0, 0.0).astype(BF16)
         low_rows = lax.dot_general(
             hit, low_all[...], (((0,), (0,)), ((), ())), preferred_element_type=F32
         )
-        copies = jnp.dot(low_rows.astype(BF16), spread, preferred_element_type=F32)
-        wide = jnp.where(of_column == low_rows[:, rank:rank + 1], copies, 0.0).astype(BF16)
-        return acc[pl.ds(first, chunk), :] + jnp.dot(wide, uw[...], preferred_element_type=F32)
-
-    def out_copy(d, c):
-        return pltpu.make_async_remote_copy(
-            src_ref=sbuf.at[d - 1, c], dst_ref=rbuf.at[d - 1, c],
-            send_sem=out_s.at[d, c], recv_sem=out_r.at[d, c],
-            device_id={"mp": lax.rem(m + d, parts)}, device_id_type=MESH,
-        )
-
-    pieces = share // chunk
-    for d in range(1, parts):
-        to = lax.rem(m + d, parts)
-        for c in range(pieces):
-            sbuf[d - 1, c] = finished(pl.multiple_of(to * share + c * chunk, chunk)).astype(BF16)
-            out_copy(d, c).start()
-    for c in range(pieces):
-        first = pl.multiple_of(m * share + c * chunk, chunk)
-        acc[pl.ds(first, chunk), :] = finished(first)
+        value = acc[pl.ds(first, chunk), :]
+        for d in range(parts):
+            ranks = lax.rem(m - d + parts, parts) * rank_portion
+            spread = jnp.where(iota(wide_shape, 0) == ranks + within, 1.0, 0.0).astype(BF16)
+            copies = jnp.dot(low_rows.astype(BF16), spread, preferred_element_type=F32)
+            wide = jnp.where(of_column == low_rows[:, rank:rank + 1], copies, 0.0).astype(BF16)
+            value = value + jnp.dot(wide, uw[d], preferred_element_type=F32)
+        acc[pl.ds(first, chunk), :] = value
     for c in range(pieces):
         value = acc[pl.ds(pl.multiple_of(m * share + c * chunk, chunk), chunk), :]
         for d in range(1, parts):
-            out_copy(d, c).wait_recv()
-            value = value + rbuf[d - 1, c].astype(F32)
+            for i in range(c * chunk // (2 * home), (c + 1) * chunk // (2 * home)):
+                out_copy(i, lax.rem(m + d, parts), d).wait_recv()
+            value = value + rbuf[d - 1, c * chunk:(c + 1) * chunk, :].astype(F32)
         out[c * chunk:(c + 1) * chunk, :] = value.astype(BF16)
 
     for h in range(2):
@@ -271,8 +303,10 @@
     each_peer(lambda d: low_copy(d).wait_send())
     for d in range(1, parts):
         part_copy(d).wait_send()
-        for c in range(pieces):
-            out_copy(d, c).wait_send()
+        up_copy(d).wait_send()
+        to = lax.rem(m + d, parts)
+        for i in range(part_chips):
+            out_copy(to * part_chips + i, to, d).wait_send()
 
 
 def solution(mesh):
@@ -287,7 +321,8 @@
         total = owners * home
         mine = CAP * owners
         share = total // parts
-        pieces = share // 128
+        some = mine // parts
+        chips = owners // 2
         far = owners // 4
         any_space = pl.BlockSpec(memory_space=pl.ANY)
         in_vmem = pl.BlockSpec(memory_space=pltpu.VMEM)
@@ -301,18 +336,18 @@
             scratch_shapes=[
                 pltpu.VMEM((total, features), BF16),
                 pltpu.VMEM((features, width), BF16),
-                pltpu.VMEM((features, rank), BF16),
-                pltpu.VMEM((owners * rank_portion, width), BF16),
+                pltpu.VMEM((rank, features), BF16),
+                pltpu.VMEM((parts, owners * rank_portion, width), BF16),
                 pltpu.VMEM((total, width), F32),
                 pltpu.VMEM((total, rank), F32),
                 pltpu.VMEM((owners, 8, 128), F32),
                 pltpu.VMEM((8, total), F32),
                 pltpu.VMEM((mine, rank), F32),
-                pltpu.VMEM((parts - 1, mine, rank), F32),
-                pltpu.VMEM((mine, 128), BF16),
-                pltpu.VMEM((owners * mine, 128), BF16),
-                pltpu.VMEM((parts - 1, pieces, 128, width), BF16),
-                pltpu.VMEM((parts - 1, pieces, 128, width), BF16),
+                pltpu.VMEM((parts - 1, some, rank), F32),
+                pltpu.VMEM((some, 128), BF16),
+                pltpu.VMEM((owners * some, 128), BF16),
+                pltpu.VMEM((chips, 2 * home, width), BF16),
+                pltpu.VMEM((parts - 1, share, width), BF16),
                 dma((4,)),
                 dma((2, far + 1, 2)),
                 dma((2, far + 1, 2)),
@@ -324,8 +359,10 @@
                 dma((parts,)),
                 dma((owners,)),
                 dma((owners,)),
-                dma((parts, pieces)),
-                dma((parts, pieces)),
+                dma((chips,)),
+                dma((parts - 1, chips // parts)),
+                dma((parts,)),
+                dma((parts,)),
             ],
             compiler_params=pltpu.CompilerParams(
                 collective_id=0, has_side_effects=True, vmem_limit_bytes=56 * 1024 * 1024
@@ -335,9 +372,9 @@
             ),
         )(
             rows,
-            request_adapter_index,
+            request_adapter_index.reshape(1, home),
             base_up_matrix,
-            adapter_down_weight.reshape(features, rank),
+            jnp.swapaxes(adapter_down_weight, 1, 2).reshape(rank, features),
             adapter_up_weight.reshape(owners * rank_portion, width),
         )
 

time: 60.3 us -> 50 us (0.83)
  Pallas kernels: 54.5 us -> 48 us
  local copies, waits for them, and re-layouts: 5.54 us -> 1.82 us
    pallas_call x1, Pallas kernels: 54.5 us -> 48 us  [body(): pl.pallas_call(functools.partial(kernel, (owners, parts, folded)), out_sh...]
    unnamed x3 -> x1, local copies, waits for them, and re-layouts: 5.54 us -> 1.82 us
where the time goes in v2:
time: 50 us; the launch traced here: 49.8 us
  Pallas kernels  48 us (96%)
  local copies, waits for them, and re-layouts  1.82 us (4%)
    pallas_call x1, Pallas kernels, body(): pl.pallas_call(functools.partial(kernel, (owners, parts, folded)), out_sh...  48 us
    unnamed x1, local copies, waits for them, and re-layouts  1.82 us

profile of v2, /device:TPU:0, one launch (start us, length us, event | category | flops | bytes accessed | tf_op | source)
XLA Modules:
  0.0 49.8 jit_solution(4489159365027176891)
XLA Ops:
  0.0 48.0 %shard_map.55 = bf16[256,896]{1,0:T(8,128)(2,1)} custom-call(bf16[32,4096]{1,0:T(8,128)(2,1)} %rows.1, s32[1,32]{1,0:T(1,128)} %bitcast.7, bf16[4096,896]{1,0:T(8,128)(2,1)} %base.1, bf16[64,4096]{1,0:T(8,128)(2,1)} %bitcast.6, bf16[512,896]{1,0:T(8,128)(2,1)} %bitcast.5), custom_call_target="tpu_custom_call" | custom-call | flops 4026531840 | bytes 7340032 | tf_op jit(solution)/shard_map/pallas_call | solution.py:331
  48.0 1.8 %copy.7 = bf16[256,896]{1,0:T(8,128)(2,1)} copy(bf16[256,896]{1,0:T(8,128)(2,1)} %shard_map.55) | data formatting | bytes 917504

commit v3 on v2

--- a/solution.py
+++ b/solution.py
@@ -211,22 +211,26 @@
                 if (k == 0 and d == 0) or (k > 0 and k <= reach(d, h)):
                     across_chip(k, d, h).wait_recv()
 
-    for k in range(1, far + 1):
-        for h in range(2):
-            for d in range(2):
-                if k <= reach(d, h):
-                    ring(k, d, h).wait_recv()
-                    if k + 1 <= reach(d, h):
-                        ring(k + 1, d, h).start()
-                    across_chip(k, d, h).start()
-        if k == 1:
-            for copy in loads[:3]:
-                copy.wait()
-        siblings_in(k - 1)
-        low_part(k - 1)
-        base_part(k - 1)
-    siblings_in(far)
-    low_part(far)
+    def arrivals(k, h):
+        for d in range(2):
+            if k <= reach(d, h):
+                ring(k, d, h).wait_recv()
+                if k + 1 <= reach(d, h):
+                    ring(k + 1, d, h).start()
+                across_chip(k, d, h).start()
+
+    def products(k):
+        siblings_in(k)
+        low_part(k)
+        base_part(k)
+
+    for copy in loads[:3]:
+        copy.wait()
+    for k in range(1, far):
+        arrivals(k, 0)
+        products(k - 1)
+        arrivals(k, 1)
+    products(far - 1)
 
     each_peer(lambda d: slot_copy(d).wait_recv())
     for q in range(total // 128):
@@ -236,6 +240,10 @@
         slot_row[:, q * 128:(q + 1) * 128] = line
     wanted = (iota((mine, total), 0) + (me * mine + 1)).astype(F32)
     pick = jnp.where(wanted == slot_row[0:1, :], 1.0, 0.0)
+    for h in range(2):
+        arrivals(far, h)
+    siblings_in(far)
+    low_part(far)
     part[...] = jnp.dot(pick, plow[...], preferred_element_type=F32, precision=lax.Precision.HIGHEST)
 
     def own_part(q):
@@ -268,20 +276,26 @@
     loads[3].wait()
     for d in range(1, parts):
         up_copy(d).wait_recv()
-    each_peer(lambda d: low_copy(d).wait_recv())
-
     pieces = share // chunk
+    spreads = []
+    for d in range(parts):
+        ranks = lax.rem(m - d + parts, parts) * rank_portion
+        spreads.append(jnp.where(iota(wide_shape, 0) == ranks + within, 1.0, 0.0).astype(BF16))
+    hits = []
     for c in range(pieces):
         first = pl.multiple_of(m * share + c * chunk, chunk)
-        hit = jnp.where(all_slots == slot_row[0:1, pl.ds(first, chunk)], 1.0, 0.0).astype(BF16)
+        line = slot_row[0:1, pl.ds(first, chunk)]
+        hits.append(jnp.where(all_slots == line, 1.0, 0.0).astype(BF16))
+    each_peer(lambda d: low_copy(d).wait_recv())
+
+    for c in range(pieces):
+        first = pl.multiple_of(m * share + c * chunk, chunk)
         low_rows = lax.dot_general(
-            hit, low_all[...], (((0,), (0,)), ((), ())), preferred_element_type=F32
+            hits[c], low_all[...], (((0,), (0,)), ((), ())), preferred_element_type=F32
         )
         value = acc[pl.ds(first, chunk), :]
         for d in range(parts):
-            ranks = lax.rem(m - d + parts, parts) * rank_portion
-            spread = jnp.where(iota(wide_shape, 0) == ranks + within, 1.0, 0.0).astype(BF16)
-            copies = jnp.dot(low_rows.astype(BF16), spread, preferred_element_type=F32)
+            copies = jnp.dot(low_rows.astype(BF16), spreads[d], preferred_element_type=F32)
             wide = jnp.where(of_column == low_rows[:, rank:rank + 1], copies, 0.0).astype(BF16)
             value = value + jnp.dot(wide, uw[d], preferred_element_type=F32)
         acc[pl.ds(first, chunk), :] = value

time: 50 us -> 47.5 us (0.950)
  Pallas kernels: 48 us -> 45.5 us
    pallas_call x1, Pallas kernels: 48 us -> 45.5 us  [body(): pl.pallas_call(functools.partial(kernel, (owners, parts, folded)), out_sh...]
where the time goes in v3:
time: 47.5 us; the launch traced here: 47.3 us
  Pallas kernels  45.5 us (96%)
  local copies, waits for them, and re-layouts  1.82 us (4%)
    pallas_call x1, Pallas kernels, body(): pl.pallas_call(functools.partial(kernel, (owners, parts, folded)), out_sh...  45.5 us
    unnamed x1, local copies, waits for them, and re-layouts  1.82 us

profile of v3, /device:TPU:0, one launch (start us, length us, event | category | flops | bytes accessed | tf_op | source)
XLA Modules:
  0.0 47.3 jit_solution(10676727372002290758)
XLA Ops:
  0.0 45.5 %shard_map.55 = bf16[256,896]{1,0:T(8,128)(2,1)} custom-call(bf16[32,4096]{1,0:T(8,128)(2,1)} %rows.1, s32[1,32]{1,0:T(1,128)} %bitcast.7, bf16[4096,896]{1,0:T(8,128)(2,1)} %base.1, bf16[64,4096]{1,0:T(8,128)(2,1)} %bitcast.6, bf16[512,896]{1,0:T(8,128)(2,1)} %bitcast.5), custom_call_target="tpu_custom_call" | custom-call | flops 4026531840 | bytes 7340032 | tf_op jit(solution)/shard_map/pallas_call | solution.py:345
  45.5 1.8 %copy.7 = bf16[256,896]{1,0:T(8,128)(2,1)} copy(bf16[256,896]{1,0:T(8,128)(2,1)} %shard_map.55) | data formatting | bytes 917504

commit v4 on v3

--- a/solution.py
+++ b/solution.py
@@ -143,9 +143,8 @@
 
         lax.fori_loop(1, owners, go, 0)
 
-    for h in range(2):
-        for d in range(2):
-            ring(1, d, h).start()
+    for d in range(2):
+        ring(1, d, 0).start()
     for h in range(2):
         across_chip(0, 0, h).start()
     each_peer(lambda d: slot_copy(d).start())
@@ -224,6 +223,9 @@
         low_part(k)
         base_part(k)
 
+    for d in range(2):
+        ring(1, d, 0).wait_send()
+        ring(1, d, 1).start()
     for copy in loads[:3]:
         copy.wait()
     for k in range(1, far):
@@ -310,7 +312,8 @@
     for h in range(2):
         for d in range(2):
             for k in range(1, reach(d, h) + 1):
-                ring(k, d, h).wait_send()
+                if k > 1 or h > 0:
+                    ring(k, d, h).wait_send()
                 across_chip(k, d, h).wait_send()
         across_chip(0, 0, h).wait_send()
     each_peer(lambda d: slot_copy(d).wait_send())

time: 47.5 us -> 47.4 us (level)
  no operation moved by 1% of the time
where the time goes in v4:
time: 47.4 us; the launch traced here: 47.3 us
  Pallas kernels  45.4 us (96%)
  local copies, waits for them, and re-layouts  1.82 us (4%)
    pallas_call x1, Pallas kernels, body(): pl.pallas_call(functools.partial(kernel, (owners, parts, folded)), out_sh...  45.4 us
    unnamed x1, local copies, waits for them, and re-layouts  1.82 us

profile of v4, /device:TPU:0, one launch (start us, length us, event | category | flops | bytes accessed | tf_op | source)
XLA Modules:
  0.0 47.3 jit_solution(7363180049650958638)
XLA Ops:
  0.0 45.4 %shard_map.55 = bf16[256,896]{1,0:T(8,128)(2,1)} custom-call(bf16[32,4096]{1,0:T(8,128)(2,1)} %rows.1, s32[1,32]{1,0:T(1,128)} %bitcast.7, bf16[4096,896]{1,0:T(8,128)(2,1)} %base.1, bf16[64,4096]{1,0:T(8,128)(2,1)} %bitcast.6, bf16[512,896]{1,0:T(8,128)(2,1)} %bitcast.5), custom_call_target="tpu_custom_call" | custom-call | flops 4026531840 | bytes 7340032 | tf_op jit(solution)/shard_map/pallas_call | solution.py:348
  45.4 1.8 %copy.7 = bf16[256,896]{1,0:T(8,128)(2,1)} copy(bf16[256,896]{1,0:T(8,128)(2,1)} %shard_map.55) | data formatting | bytes 917504
